TPU v7x, 32 devices: a whole 2x2x4 slice. The times are simulated.
32 devices in a mesh: seq: 8 (over y, x, core), exp: 4 (over z).
Axes of the slice: x: 2, y: 2, z: 4, core: 2. Of those that a mesh axis runs over, the one named last changes fastest.
Arguments:
- query_proj: bfloat16 [512, 4096], P('seq', 'exp'), may hold values from -6 to 6
- key_proj: bfloat16 [512, 4096], P('seq', 'exp'), may hold values from -6 to 6
- value_proj: bfloat16 [512, 4096], P('seq', 'exp'), may hold values from -6 to 6
- residual: bfloat16 [512, 6144], P(('seq', 'exp')), may hold values from -6 to 6
- out_weight: bfloat16 [6144, 4096], P('seq', 'exp'), may hold values from -0.09375 to 0.09375
- expert_ids: int32 [512, 2], P(('seq', 'exp')), may hold values from 0 to 3, all different within a row; in each aligned block of 16 rows (0 to 15, 16 to 31, ...) at most 12 rows name the same one
- gate_values: float32 [512, 2], P(('seq', 'exp')), may hold values from 0.2 to 1
- w_gate: bfloat16 [4, 9216, 6144], P('exp', 'seq'), may hold values from -0.078125 to 0.078125
- w_up: bfloat16 [4, 9216, 6144], P('exp', 'seq'), may hold values from -0.078125 to 0.078125
- w_down: bfloat16 [4, 9216, 6144], P('exp', 'seq'), may hold values from -0.0625 to 0.0625
Outputs:
- mixed: bfloat16 [512, 6144], P(('seq', 'exp'))
Inputs may be any that keep to these rules, and one draw needn't show every extreme that they name: `expert_ids`: within the 16 rows of one device no expert is named more than 12 times, a bound that some block reaches; the 2 experts of a row differ.
All inputs are finite; a program needn't handle non-finite values.
Results may differ from a plain program's by a relative error of at most 0.018.
Values may be sent and summed in bfloat16 or wider, within the bound.
A program may use at most 128 MiB of HBM per device.

v0:
```python
import jax
import jax.numpy as jnp
from jax import lax
from jax.sharding import PartitionSpec as P

HD = 128
TOP = 2


def entering(array, axis, combine, identity):
    devices, place = (lax.axis_size(axis), lax.axis_index(axis))
    everything = lax.all_gather(array.astype(jnp.bfloat16), axis)
    start = jnp.broadcast_to(jnp.asarray(identity, array.dtype), array.shape)

    def hop(k, before):
        reached = k < place
        new = combine(before, everything[k].astype(array.dtype))
        return jnp.where(reached, new, before)

    return lax.fori_loop(0, devices, hop, start)


def features(x):
    widened = x.astype(jnp.float32)
    return (widened * jax.nn.sigmoid(widened)).astype(jnp.bfloat16)


def times_rows(left, right):
    return lax.dot_general(
        left, right, (((1,), (1,)), ((), ())), preferred_element_type=jnp.float32
    )


def local(
    query_proj,
    key_proj,
    value_proj,
    residual,
    out_weight,
    expert_ids,
    gate_values,
    w_gate,
    w_up,
    w_down,
):
    tokens_here = query_proj.shape[0]
    heads_here = query_proj.shape[1] // HD
    query_feat = features(query_proj).reshape(tokens_here, heads_here, HD)
    key_feat = features(key_proj).reshape(tokens_here, heads_here, HD)
    value_rows = value_proj.reshape(tokens_here, heads_here, HD)
    span_state = jnp.einsum(
        "thd,the->hde", key_feat, value_rows, preferred_element_type=jnp.float32
    )
    earlier = entering(span_state, "seq", lambda a, b: a + b, jnp.zeros_like(span_state))
    prefix = earlier.astype(jnp.bfloat16)
    earlier_term = jnp.einsum(
        "thd,hde->the", query_feat, prefix, preferred_element_type=jnp.float32
    )
    scores = jnp.einsum("thd,shd->hts", query_feat, key_feat, preferred_element_type=jnp.float32)
    causal = jnp.arange(tokens_here)[:, None] >= jnp.arange(tokens_here)[None, :]
    weights = jnp.where(causal[None], scores, 0.0).astype(jnp.bfloat16)
    local_term = jnp.einsum("hts,she->the", weights, value_rows, preferred_element_type=jnp.float32)
    combined = local_term + earlier_term
    normed = combined * lax.rsqrt(jnp.mean(combined * combined, axis=-1, keepdims=True) + 1e-06)
    normed = normed.astype(jnp.bfloat16).reshape(tokens_here, heads_here * HD)
    partial_out = times_rows(normed, lax.all_gather(out_weight, "seq", axis=0, tiled=True))
    summed = lax.psum_scatter(
        partial_out.astype(jnp.bfloat16), "exp", scatter_dimension=0, tiled=True
    ).astype(jnp.float32)
    mixed_in = (residual.astype(jnp.float32) + summed).astype(jnp.bfloat16)
    groups = lax.axis_size("exp")
    tok_sub = residual.shape[0]
    capacity = max(2, (3 * tok_sub * TOP + 2 * groups - 1) // (2 * groups))
    local_rows = groups * capacity
    chosen = expert_ids.reshape(-1)
    onehot = (chosen[:, None] == jnp.arange(groups, dtype=jnp.int32)[None, :]).astype(jnp.int32)
    before = jnp.cumsum(onehot, axis=0) - onehot
    slot_index = jnp.sum(before * onehot, axis=1)
    target = chosen * capacity + slot_index
    targets = target.reshape(tok_sub, TOP)
    slot_ids = jnp.arange(local_rows, dtype=jnp.int32)
    placing = jnp.any(slot_ids[:, None, None] == targets[None, :, :], axis=2).astype(jnp.bfloat16)
    outgoing = jnp.dot(placing, mixed_in, preferred_element_type=jnp.float32).astype(jnp.bfloat16)
    outgoing = outgoing.reshape(groups, capacity, -1)
    gate_local = w_gate[0]
    up_local = w_up[0]
    down_local = w_down[0]
    hidden_here = gate_local.shape[0]
    arrived = lax.all_to_all(outgoing, "exp", split_axis=0, concat_axis=0, tiled=True).reshape(
        local_rows, -1
    )
    rows_part = lax.all_gather(arrived, "seq", axis=0, tiled=True)
    acts = jnp.concatenate(
        [times_rows(rows_part, gate_local), times_rows(rows_part, up_local)], axis=1
    )
    gate_act = acts[:, :hidden_here]
    up_act = acts[:, hidden_here:]
    activated = (jax.nn.silu(gate_act) * up_act).astype(jnp.bfloat16)
    rows_part = activated
    expert_sums = lax.psum_scatter(
        jnp.dot(rows_part, down_local, preferred_element_type=jnp.float32).astype(jnp.bfloat16),
        "seq",
        scatter_dimension=0,
        tiled=True,
    )
    expert_out = expert_sums.reshape(groups, capacity, -1)
    returned = lax.all_to_all(expert_out, "exp", split_axis=0, concat_axis=0, tiled=True).reshape(
        local_rows, -1
    )
    picked = returned[target].astype(jnp.float32).reshape(tok_sub, TOP, -1)
    mixed = mixed_in.astype(jnp.float32) + jnp.sum(gate_values[:, :, None] * picked, axis=1)
    return mixed.astype(jnp.bfloat16)


def solution(mesh):
    return jax.shard_map(
        local,
        mesh=mesh,
        in_specs=(
            P("seq", "exp"),
            P("seq", "exp"),
            P("seq", "exp"),
            P(("seq", "exp"), None),
            P("seq", "exp"),
            P(("seq", "exp"), None),
            P(("seq", "exp"), None),
            P("exp", "seq", None),
            P("exp", "seq", None),
            P("exp", "seq", None),
        ),
        out_specs=P(("seq", "exp"), None),
        check_vma=False,
    )
```

profile of v0, /device:TPU:0, one launch (start us, length us, event | category | flops | bytes accessed | tf_op | source)
XLA Modules:
  0.0 334.6 jit_solution(14853857434425266002)
XLA Ops:
  6.5 1.1 fusion.35
  7.7 1.0 convolution_convert_fusion.2
  8.8 0.7 all-gather.5.cloned.1.call-update
  9.6 0.3 convolution_bitcast_fusion.1
  9.9 30.0 %all-gather.9.cloned.1.call-done = bf16[64,128,128]{2,1,0:T(8,128)(2,1)} async-done(((bf16[8,128,128]{2,1,0:T(8,128)(2,1)}), bf16[64,128,128]{2,1,0:T(8,128)(2,1)}) %all-gather.9.cloned.1.call-update) | async-done | bytes 2097168 | tf_op jit(solution)/shard_map/all_gather | solution.py:12
  39.9 10.1 %while.14 = (s32[]{:T(128)}, f32[8,128,128]{2,1,0:T(8,128)S(1)}, s32[]{:T(128)}, bf16[8,8,128,128]{3,2,1,0:T(8,128)(2,1)}, s32[]{:T(128)}, /*index=5*/s32[]{:T(128)}) while((s32[]{:T(128)}, f32[8,128,128]{2,1,0:T(8,128)S(1)}, s32[]{:T(128)}, bf16[8,8,128,128]{3,2,1,0:T(8,128)(2,1)}, s32[]{:T(128)}, /*index=5*/s32[]{:T(128)}) %tuple.48), condition=%wide.region_1.2_spmd.clone, body=%wide.region_0.1_spmd.clone.sunk | while | flops 524292 | bytes 1310813 | solution.py:20
  39.9 1.2 add_select_fusion.2
  41.1 1.2 add_select_fusion.2
  42.4 1.2 add_select_fusion.2
  43.6 1.2 add_select_fusion.2
  44.9 1.2 add_select_fusion.2
  46.2 1.2 add_select_fusion.2
  47.4 1.3 add_select_fusion.2
  48.7 1.3 add_select_fusion.2
  50.3 63.6 %all-gather.5.cloned.1.call-done = bf16[6144,1024]{1,0:T(8,128)(2,1)} async-done(((bf16[768,1024]{1,0:T(8,128)(2,1)}), bf16[6144,1024]{1,0:T(8,128)(2,1)}) %all-gather.5.cloned.1.call-update) | async-done | bytes 12582928 | tf_op jit(solution)/shard_map/all_gather | solution.py:66
  113.9 9.5 %convolution_convert_fusion = bf16[64,6144]{1,0:T(8,128)(2,1)} fusion(bf16[6144,1024]{1,0:T(8,128)(2,1)} %all-gather.5.cloned.1.call-done, f32[64,8,128]{2,0,1:T(8,128)S(1)} %get-tuple-element.111, f32[64,8]{0,1:T(8,128)S(1)} %add_rsqrt_fusion), kind=kOutput, calls=%fused_computation.9 | convolution fusion | flops 805830656 | bytes 13633536 | tf_op jit(solution)/shard_map/dot_general | solution.py:29
  124.1 0.6 broadcast_multiply_fusion
  124.9 22.0 %reduce-scatter.3.cloned.1.call-done = bf16[16,6144]{1,0:T(8,128)(2,1)} async-done(((bf16[64,6144]{1,0:T(8,128)(2,1)}), bf16[16,6144]{1,0:T(8,128)(2,1)}) %reduce-scatter.3.cloned.1.call-update) | async-done | bytes 196624 | tf_op jit(solution)/shard_map/reduce_scatter | solution.py:67
  146.9 1.3 convolution_convert_fusion.1
  148.4 22.6 %all_to_all.10 = bf16[4,12,6144]{2,1,0:T(8,128)(2,1)S(1)} all-to-all(bf16[4,12,6144]{2,1,0:T(8,128)(2,1)S(1)} %reshape.91), channel_id=1, replica_groups=mesh['seq'=8,'exp'=4] {'exp'}, dimensions={0} | all-to-all | bytes 1179648 | tf_op jit(solution)/shard_map/all_to_all | solution.py:89
  170.9 1.0 reshape.92
  172.1 37.9 %all-gather.7.cloned.1.call-done = bf16[384,6144]{1,0:T(8,128)(2,1)} async-done(((bf16[48,6144]{1,0:T(8,128)(2,1)}), bf16[384,6144]{1,0:T(8,128)(2,1)}) %all-gather.7.cloned.1.call-update) | async-done | bytes 4718608 | tf_op jit(solution)/shard_map/all_gather | solution.py:92
  210.1 10.2 %fusion.4 = f32[384,1152]{1,0:T(8,128)S(1)} fusion(bf16[384,6144]{1,0:T(8,128)(2,1)} %all-gather.7.cloned.1.call-done, bf16[1,1152,6144]{2,1,0:T(8,128)(2,1)} %param.19), kind=kOutput, calls=%fused_computation.6 | convolution fusion | flops 5435817984 | bytes 20643840 | tf_op jit(solution)/shard_map/dot_general | solution.py:29
  220.3 23.4 %fusion.6 = bf16[384,6144]{1,0:T(8,128)(2,1)} fusion(bf16[1,1152,6144]{2,1,0:T(8,128)(2,1)} %param.21, bf16[384,6144]{1,0:T(8,128)(2,1)} %all-gather.7.cloned.1.call-done, bf16[1,1152,6144]{2,1,0:T(8,128)(2,1)} %param.20, f32[384,1152]{1,0:T(8,128)S(1)} %fusion.4), kind=kOutput, calls=%fused_computation.8 | convolution fusion | flops 10876649472 | bytes 39518208 | tf_op jit(solution)/shard_map/dot_general | solution.py:101
  243.8 54.1 %reduce-scatter.5.cloned.1.call-done = bf16[48,6144]{1,0:T(8,128)(2,1)} async-done(((bf16[384,6144]{1,0:T(8,128)(2,1)}), bf16[48,6144]{1,0:T(8,128)(2,1)}) %reduce-scatter.5.cloned.1.call-update) | async-done | bytes 589840 | tf_op jit(solution)/shard_map/reduce_scatter | solution.py:100
  297.9 2.1 reshape.93
  300.0 4.7 %all-to-all-start.1 = ((bf16[4,12,6144]{2,1,0:T(8,128)(2,1)}), bf16[4,12,6144]{2,1,0:T(8,128)(2,1)S(1)}, u32[]{:S(2)}, u32[]{:S(2)}) async-start(bf16[4,12,6144]{2,1,0:T(8,128)(2,1)} %reshape.93), calls=%async_computation.3 | async-start | bytes 1572864 | tf_op jit(solution)/shard_map/all_to_all | solution.py:107
  304.9 19.9 %all-to-all-done.1 = bf16[4,12,6144]{2,1,0:T(8,128)(2,1)S(1)} async-done(((bf16[4,12,6144]{2,1,0:T(8,128)(2,1)}), bf16[4,12,6144]{2,1,0:T(8,128)(2,1)S(1)}, u32[]{:S(2)}, u32[]{:S(2)}) %all-to-all-start.1) | async-done | bytes 589856 | tf_op jit(solution)/shard_map/all_to_all | solution.py:107
  325.0 0.8 gather_fusion
  325.8 0.5 reshape.96
  326.3 1.1 multiply_reduce_fusion
  327.4 0.7 add_convert_fusion
  (47 shorter events, 1.9 us)
Async XLA Ops:
  6.5 1.2 copy-start
  6.5 33.3 %all-gather.9.cloned.1.call-start = ((), (), s32[]{:S(2)}) async-start(), calls=%async_computation.8 | async-start | bytes 2359296 | tf_op jit(solution)/shard_map/all_gather | solution.py:12
  8.7 105.2 %all-gather.5.cloned.1.call-start = ((), (), s32[]{:S(2)}) async-start(), calls=%async_computation.4 | async-start | bytes 14155776 | tf_op jit(solution)/shard_map/all_gather | solution.py:66
  9.5 137.4 %reduce-scatter.3.cloned.1.call-start = ((), (), s32[]{:S(2)}) async-start(), calls=%async_computation.5 | async-start | bytes 983040 | tf_op jit(solution)/shard_map/reduce_scatter | solution.py:67
  113.9 9.6 %copy-start.8 = (s32[16,2]{0,1:T(2,128)S(1)}, s32[16,2]{0,1:T(2,128)}, u32[]{:S(2)}) copy-start(s32[16,2]{0,1:T(2,128)} %param.17) | copy-start | bytes 388
  113.9 33.0 %copy-start.2 = (bf16[16,6144]{1,0:T(8,128)(2,1)S(1)}, bf16[16,6144]{1,0:T(8,128)(2,1)}, u32[]{:S(2)}) copy-start(bf16[16,6144]{1,0:T(8,128)(2,1)} %param.15) | copy-start | bytes 589828
  123.5 86.6 %all-gather.7.cloned.1.call-start = ((), (), s32[]{:S(2)}) async-start(), calls=%async_computation.6 | async-start | bytes 5308416 | tf_op jit(solution)/shard_map/all_gather | solution.py:92
  124.0 96.3 %copy-start.6 = (s32[32]{0:T(128)}, s32[32]{0:T(128)S(1)}, u32[]{:S(2)}) copy-start(s32[32]{0:T(128)S(1)} %select_reduce_fusion) | copy-start | bytes 388
  171.9 125.9 %reduce-scatter.5.cloned.1.call-start = ((), (), s32[]{:S(2)}) async-start(), calls=%async_computation.7 | async-start | bytes 5308416 | tf_op jit(solution)/shard_map/reduce_scatter | solution.py:100
  243.8 60.9 %copy-start.5 = (s32[16,2]{1,0:T(8,128)S(1)}, s32[16,2]{1,0:T(8,128)}, u32[]{:S(2)}) copy-start(s32[16,2]{1,0:T(8,128)} %get-tuple-element.108) | copy-start | bytes 388
  243.8 61.0 %copy-start.9 = (f32[16,2]{0,1:T(2,128)S(1)}, f32[16,2]{0,1:T(2,128)}, u32[]{:S(2)}) copy-start(f32[16,2]{0,1:T(2,128)} %param.18) | copy-start | bytes 388
  243.8 61.1 %copy-start.7 = (s32[32]{0:T(128)S(1)}, s32[32]{0:T(128)}, u32[]{:S(2)}) copy-start(s32[32]{0:T(128)} %copy-done.6) | copy-start | bytes 388
  297.9 30.2 %copy-start.1 = (bf16[64,1024]{1,0:T(8,128)(2,1)S(1)}, bf16[64,1024]{1,0:T(8,128)(2,1)}, u32[]{:S(2)}) copy-start(bf16[64,1024]{1,0:T(8,128)(2,1)} %param.14) | copy-start | bytes 393220
  300.0 27.4 %copy-start.3 = (bf16[16,6144]{1,0:T(8,128)(2,1)S(1)}, bf16[16,6144]{1,0:T(8,128)(2,1)}, u32[]{:S(2)}) copy-start(bf16[16,6144]{1,0:T(8,128)(2,1)} %param.15) | copy-start | bytes 589828
  300.0 27.4 %copy-start.4 = (bf16[16,6144]{1,0:T(8,128)(2,1)S(1)}, bf16[16,6144]{1,0:T(8,128)(2,1)}, u32[]{:S(2)}) copy-start(bf16[16,6144]{1,0:T(8,128)(2,1)} %reduce-scatter.3.cloned.1.call-done) | copy-start | bytes 589828
  300.0 24.8 %all-to-all-start.1 = ((bf16[4,12,6144]{2,1,0:T(8,128)(2,1)}), bf16[4,12,6144]{2,1,0:T(8,128)(2,1)S(1)}, u32[]{:S(2)}, u32[]{:S(2)}) async-start(bf16[4,12,6144]{2,1,0:T(8,128)(2,1)} %reshape.93), calls=%async_computation.3 | async-start | bytes 1572864 | tf_op jit(solution)/shard_map/all_to_all | solution.py:107
Sparse Core Ops, SparseCore 0:
  9.2 30.5 all-gather.8
  41.8 72.1 all-gather.4
  123.6 23.2 reduce-scatter.2
  172.0 38.0 all-gather.6
  243.9 53.8 reduce-scatter.4
where the time goes:
time: 335 us
  waiting for transfers between devices  228 us (68%)
  matrix products  46.1 us (14%)
  blocking collectives  22.6 us (7%)
  other arithmetic  14 us (4%)
  between operations  13.3 us (4%)
  local copies, waits for them, and re-layouts  5.18 us (2%)
  starting transfers between devices  5.07 us (2%)
    all_gather x1, waiting for transfers between devices, local(): lax.all_gather(out_weight, 'seq', axis=0, tiled=True)  63.6 us
    reduce_scatter x1, waiting for transfers between devices, local(): lax.psum_scatter(jnp.dot(rows_part, down_local, preferred_element_type=jn...  54.1 us
    all_gather x1, waiting for transfers between devices, local(): rows_part = lax.all_gather(arrived, 'seq', axis=0, tiled=True)  37.9 us
    all_gather x1, waiting for transfers between devices, entering(): everything = lax.all_gather(array.astype(jnp.bfloat16), axis)  30 us
    dot_general x1, matrix products, local(): jnp.dot(rows_part, down_local, preferred_element_type=jnp.float32)  23.4 us
    all_to_all x1, blocking collectives, local(): lax.all_to_all(outgoing, 'exp', split_axis=0, concat_axis=0, tiled=True)  22.6 us
    reduce_scatter x1, waiting for transfers between devices, local(): lax.psum_scatter(partial_out.astype(jnp.bfloat16), 'exp', scatter_dimensi...  22 us
    all_to_all x1, waiting for transfers between devices, local(): lax.all_to_all(expert_out, 'exp', split_axis=0, concat_axis=0, tiled=True)  19.9 us
  transfers between devices with their start and end apart: 6, of which 6 were waited for; matrix products, arithmetic and copies ran while one was open for 4% of the time, Pallas kernels for 0%

commit v1 on v0

--- a/solution.py
+++ b/solution.py
@@ -5,6 +5,22 @@
 
 HD = 128
 TOP = 2
+
+
+def gather_around(x, axis, dim):
+    ways, here, step = (lax.axis_size(axis), lax.axis_index(axis), x.shape[dim])
+    shape = [n * ways if d == dim else n for d, n in enumerate(x.shape)]
+    full = lax.dynamic_update_slice_in_dim(jnp.zeros(shape, x.dtype), x, here * step, axis=dim)
+    going_up = going_down = x
+    for far in range(1, ways // 2 + 1):
+        going_up = lax.ppermute(going_up, axis, [(d, (d + 1) % ways) for d in range(ways)])
+        full = lax.dynamic_update_slice_in_dim(full, going_up, (here - far) % ways * step, axis=dim)
+        if 2 * far < ways:
+            going_down = lax.ppermute(going_down, axis, [(d, (d - 1) % ways) for d in range(ways)])
+            full = lax.dynamic_update_slice_in_dim(
+                full, going_down, (here + far) % ways * step, axis=dim
+            )
+    return full
 
 
 def entering(array, axis, combine, identity):
@@ -63,7 +79,7 @@
     combined = local_term + earlier_term
     normed = combined * lax.rsqrt(jnp.mean(combined * combined, axis=-1, keepdims=True) + 1e-06)
     normed = normed.astype(jnp.bfloat16).reshape(tokens_here, heads_here * HD)
-    partial_out = times_rows(normed, lax.all_gather(out_weight, "seq", axis=0, tiled=True))
+    partial_out = times_rows(normed, gather_around(out_weight, "seq", 0))
     summed = lax.psum_scatter(
         partial_out.astype(jnp.bfloat16), "exp", scatter_dimension=0, tiled=True
     ).astype(jnp.float32)

time: 335 us -> 366 us (1.093)
  local copies, waits for them, and re-layouts: 5.18 us -> 30.1 us
  starting transfers between devices: 5.07 us -> 14.2 us
    ppermute x0 -> x7, waiting for transfers between devices: none -> 87.1 us  [the longest x4 73.2 us: gather_around(): lax.ppermute(going_up, axis, [(d, (d + 1) % ways) for d in range(ways)])]
    all_gather x1 -> x0, waiting for transfers between devices: 63.6 us -> none  [local(): lax.all_gather(out_weight, 'seq', axis=0, tiled=True)]
    all_gather x1, waiting for transfers between devices: 30 us -> 0.01 us  [entering(): everything = lax.all_gather(array.astype(jnp.bfloat16), axis)]
    dynamic_update_slice x0 -> x8, local copies, waits for them, and re-layouts: none -> 18.7 us  [the longest x4 10.8 us: gather_around(): lax.dynamic_update_slice_in_dim(full, going_up, (here - far) % ways * ste...]
    ppermute x0 -> x7, starting transfers between devices: none -> 9.32 us  [the longest x3 8.45 us: gather_around(): lax.ppermute(going_down, axis, [(d, (d - 1) % ways) for d in range(ways)])]
    broadcast_in_dim x0 -> x1, local copies, waits for them, and re-layouts: none -> 6.14 us  [gather_around(): jnp.zeros(shape, x.dtype)]
  transfers between devices with their start and end apart: 6 -> 12, of which waited for: 6 -> 10; matrix products, arithmetic and copies ran while one was open for 4% -> 10% of each run, Pallas kernels for 0% -> 0%
where the time goes in v1:
time: 366 us; the launch traced here: 365 us
  waiting for transfers between devices  225 us (61%)
  matrix products  46.1 us (13%)
  local copies, waits for them, and re-layouts  30.1 us (8%)
  blocking collectives  22.6 us (6%)
  starting transfers between devices  14.2 us (4%)
  other arithmetic  13.9 us (4%)
  between operations  13.3 us (4%)
    ppermute x4, waiting for transfers between devices, gather_around(): lax.ppermute(going_up, axis, [(d, (d + 1) % ways) for d in range(ways)])  73.2 us
    reduce_scatter x1, waiting for transfers between devices, local(): lax.psum_scatter(jnp.dot(rows_part, down_local, preferred_element_type=jn...  54.1 us
    all_gather x1, waiting for transfers between devices, local(): rows_part = lax.all_gather(arrived, 'seq', axis=0, tiled=True)  37.9 us
    reduce_scatter x1, waiting for transfers between devices, local(): lax.psum_scatter(partial_out.astype(jnp.bfloat16), 'exp', scatter_dimensi...  25.5 us
    dot_general x1, matrix products, local(): jnp.dot(rows_part, down_local, preferred_element_type=jnp.float32)  23.4 us
    all_to_all x1, blocking collectives, local(): lax.all_to_all(outgoing, 'exp', split_axis=0, concat_axis=0, tiled=True)  22.6 us
    all_to_all x1, waiting for transfers between devices, local(): lax.all_to_all(expert_out, 'exp', split_axis=0, concat_axis=0, tiled=True)  19.9 us
    dot_general x2, matrix products, times_rows(): lax.dot_general(left, right, (((1,), (1,)), ((), ())), preferred_element_...  19.7 us
  transfers between devices with their start and end apart: 12, of which 10 were waited for; matrix products, arithmetic and copies ran while one was open for 10% of the time, Pallas kernels for 0%

profile of v1, /device:TPU:0, one launch (start us, length us, event | category | flops | bytes accessed | tf_op | source)
XLA Modules:
  0.0 364.8 jit_solution(7598408187239935435)
XLA Ops:
  9.3 3.0 collective-permute-start.1
  12.3 36.5 %collective-permute-done = bf16[768,1024]{1,0:T(8,128)(2,1)} collective-permute-done((bf16[768,1024]{1,0:T(8,128)(2,1)}, bf16[768,1024]{1,0:T(8,128)(2,1)}, u32[]{:S(2)}, u32[]{:S(2)}) %collective-permute-start) | collective-permute-done | bytes 1572896 | tf_op jit(solution)/shard_map/ppermute | solution.py:16
  49.1 3.4 collective-permute-done.1
  52.5 2.8 collective-permute-start.3
  55.3 28.0 %collective-permute-done.2 = bf16[768,1024]{1,0:T(8,128)(2,1)} collective-permute-done((bf16[768,1024]{1,0:T(8,128)(2,1)}, bf16[768,1024]{1,0:T(8,128)(2,1)}, u32[]{:S(2)}, u32[]{:S(2)}) %collective-permute-start.2) | collective-permute-done | bytes 1572896 | tf_op jit(solution)/shard_map/ppermute | solution.py:16
  83.3 6.1 %broadcast_in_dim.29 = bf16[6144,1024]{1,0:T(8,128)(2,1)} broadcast(bf16[]{:T(256)} %constant.95.clone.1), dimensions={} | broadcast | bytes 12582914 | tf_op jit(solution)/shard_map/broadcast_in_dim | solution.py:13
  89.5 1.3 constant_dynamic-update-slice_fusion.7
  91.1 2.7 constant_dynamic-update-slice_fusion.6
  93.8 2.7 constant_dynamic-update-slice_fusion.5
  96.4 2.6 collective-permute-start.5
  99.1 2.7 constant_dynamic-update-slice_fusion.4
  101.8 2.7 constant_dynamic-update-slice_fusion.3
  104.4 2.9 collective-permute-done.4
  107.3 10.0 %while.14 = (s32[]{:T(128)}, f32[8,128,128]{2,1,0:T(8,128)S(1)}, s32[]{:T(128)}, bf16[8,8,128,128]{3,2,1,0:T(8,128)(2,1)}, s32[]{:T(128)}, /*index=5*/s32[]{:T(128)}) while((s32[]{:T(128)}, f32[8,128,128]{2,1,0:T(8,128)S(1)}, s32[]{:T(128)}, bf16[8,8,128,128]{3,2,1,0:T(8,128)(2,1)}, s32[]{:T(128)}, /*index=5*/s32[]{:T(128)}) %tuple.46), condition=%wide.region_1.2_spmd.clone, body=%wide.region_0.1_spmd.clone.sunk | while | flops 524292 | bytes 1310813 | solution.py:36
  108.5 1.2 add_select_fusion.2
  109.8 1.2 add_select_fusion.2
  117.6 2.8 constant_dynamic-update-slice_fusion.2
  120.4 10.5 %collective-permute-done.5 = bf16[768,1024]{1,0:T(8,128)(2,1)S(1)} collective-permute-done((bf16[768,1024]{1,0:T(8,128)(2,1)}, bf16[768,1024]{1,0:T(8,128)(2,1)S(1)}, u32[]{:S(2)}, u32[]{:S(2)}) %collective-permute-start.5) | collective-permute-done | bytes 1572896 | tf_op jit(solution)/shard_map/ppermute | solution.py:19
  130.9 1.3 constant_dynamic-update-slice_fusion.1
  132.2 5.9 %collective-permute-done.6 = bf16[768,1024]{1,0:T(8,128)(2,1)} collective-permute-done((bf16[768,1024]{1,0:T(8,128)(2,1)}, bf16[768,1024]{1,0:T(8,128)(2,1)}, u32[]{:S(2)}, u32[]{:S(2)}) %collective-permute-start.6) | collective-permute-done | bytes 1572896 | tf_op jit(solution)/shard_map/ppermute | solution.py:16
  138.1 2.7 constant_dynamic-update-slice_fusion
  140.8 9.5 %convolution_convert_fusion = bf16[64,6144]{1,0:T(8,128)(2,1)} fusion(bf16[6144,1024]{1,0:T(8,128)(2,1)} %constant_dynamic-update-slice_fusion, f32[64,8,128]{2,0,1:T(8,128)S(1)} %get-tuple-element.111, f32[64,8]{0,1:T(8,128)S(1)} %add_rsqrt_fusion), kind=kOutput, calls=%fused_computation.9 | convolution fusion | flops 805830656 | bytes 13633536 | tf_op jit(solution)/shard_map/dot_general | solution.py:45
  151.7 25.5 %reduce-scatter.3.cloned.1.call-done = bf16[16,6144]{1,0:T(8,128)(2,1)} async-done(((bf16[64,6144]{1,0:T(8,128)(2,1)}), bf16[16,6144]{1,0:T(8,128)(2,1)}) %reduce-scatter.3.cloned.1.call-update) | async-done | bytes 196624 | tf_op jit(solution)/shard_map/reduce_scatter | solution.py:83
  177.2 1.3 convolution_convert_fusion.1
  178.7 22.6 %all_to_all.10 = bf16[4,12,6144]{2,1,0:T(8,128)(2,1)S(1)} all-to-all(bf16[4,12,6144]{2,1,0:T(8,128)(2,1)S(1)} %reshape.91), channel_id=1, replica_groups=mesh['seq'=8,'exp'=4] {'exp'}, dimensions={0} | all-to-all | bytes 1179648 | tf_op jit(solution)/shard_map/all_to_all | solution.py:105
  202.4 37.9 %all-gather.4.cloned.1.call-done = bf16[384,6144]{1,0:T(8,128)(2,1)} async-done(((bf16[48,6144]{1,0:T(8,128)(2,1)}), bf16[384,6144]{1,0:T(8,128)(2,1)}) %all-gather.4.cloned.1.call-update) | async-done | bytes 4718608 | tf_op jit(solution)/shard_map/all_gather | solution.py:108
  240.3 10.3 %fusion.4 = f32[384,1152]{1,0:T(8,128)S(1)} fusion(bf16[384,6144]{1,0:T(8,128)(2,1)} %all-gather.4.cloned.1.call-done, bf16[1,1152,6144]{2,1,0:T(8,128)(2,1)} %param.19), kind=kOutput, calls=%fused_computation.6 | convolution fusion | flops 5435817984 | bytes 20643840 | tf_op jit(solution)/shard_map/dot_general | solution.py:45
  250.7 23.4 %fusion.6 = bf16[384,6144]{1,0:T(8,128)(2,1)} fusion(bf16[1,1152,6144]{2,1,0:T(8,128)(2,1)} %param.21, bf16[384,6144]{1,0:T(8,128)(2,1)} %all-gather.4.cloned.1.call-done, bf16[1,1152,6144]{2,1,0:T(8,128)(2,1)} %param.20, f32[384,1152]{1,0:T(8,128)S(1)} %fusion.4), kind=kOutput, calls=%fused_computation.8 | convolution fusion | flops 10876649472 | bytes 39518208 | tf_op jit(solution)/shard_map/dot_general | solution.py:117
  274.1 54.1 %reduce-scatter.5.cloned.1.call-done = bf16[48,6144]{1,0:T(8,128)(2,1)} async-done(((bf16[384,6144]{1,0:T(8,128)(2,1)}), bf16[48,6144]{1,0:T(8,128)(2,1)}) %reduce-scatter.5.cloned.1.call-update) | async-done | bytes 589840 | tf_op jit(solution)/shard_map/reduce_scatter | solution.py:116
  328.2 2.1 reshape.93
  330.3 4.6 %all-to-all-start.1 = ((bf16[4,12,6144]{2,1,0:T(8,128)(2,1)}), bf16[4,12,6144]{2,1,0:T(8,128)(2,1)S(1)}, u32[]{:S(2)}, u32[]{:S(2)}) async-start(bf16[4,12,6144]{2,1,0:T(8,128)(2,1)} %reshape.93), calls=%async_computation.3 | async-start | bytes 1572864 | tf_op jit(solution)/shard_map/all_to_all | solution.py:123
  335.1 19.9 %all-to-all-done.1 = bf16[4,12,6144]{2,1,0:T(8,128)(2,1)S(1)} async-done(((bf16[4,12,6144]{2,1,0:T(8,128)(2,1)}), bf16[4,12,6144]{2,1,0:T(8,128)(2,1)S(1)}, u32[]{:S(2)}, u32[]{:S(2)}) %all-to-all-start.1) | async-done | bytes 589856 | tf_op jit(solution)/shard_map/all_to_all | solution.py:123
  (69 shorter events, 17.3 us)
Async XLA Ops:
  6.5 1.7 copy-start
  6.5 82.9 %copy-start.2 = (bf16[768,1024]{1,0:T(8,128)(2,1)S(1)}, bf16[768,1024]{1,0:T(8,128)(2,1)}, u32[]{:S(2)}) copy-start(bf16[768,1024]{1,0:T(8,128)(2,1)} %param.16) | copy-start | bytes 4718596
  6.5 100.7 %all-gather.6.cloned.1.call-start = ((), (), s32[]{:S(2)}) async-start(), calls=%async_computation.7 | async-start | bytes 2359296 | tf_op jit(solution)/shard_map/all_gather | solution.py:28
  6.5 42.2 %collective-permute-start = (bf16[768,1024]{1,0:T(8,128)(2,1)}, bf16[768,1024]{1,0:T(8,128)(2,1)}, u32[]{:S(2)}, u32[]{:S(2)}) collective-permute-start(bf16[768,1024]{1,0:T(8,128)(2,1)} %param.16), channel_id=1, source_target_pairs={{0,4},{4,8},{8,12},{12,16},{16,20},{20,24},{24,28},{28,0},{1,5},{5... | collective-permute-start | bytes 4718600 | tf_op jit(solution)/shard_map/ppermute | solution.py:16
  9.2 168.0 %reduce-scatter.3.cloned.1.call-start = ((), (), s32[]{:S(2)}) async-start(), calls=%async_computation.4 | async-start | bytes 983040 | tf_op jit(solution)/shard_map/reduce_scatter | solution.py:83
  9.3 43.2 %collective-permute-start.1 = (bf16[768,1024]{1,0:T(8,128)(2,1)}, bf16[768,1024]{1,0:T(8,128)(2,1)}, u32[]{:S(2)}, u32[]{:S(2)}) collective-permute-start(bf16[768,1024]{1,0:T(8,128)(2,1)} %param.16), channel_id=1, source_target_pairs={{0,28},{4,0},{8,4},{12,8},{16,12},{20,16},{24,20},{28,24},{1,29},{... | collective-permute-start | bytes 4718600 | tf_op jit(solution)/shard_map/ppermute | solution.py:19
  48.7 34.6 %collective-permute-start.2 = (bf16[768,1024]{1,0:T(8,128)(2,1)}, bf16[768,1024]{1,0:T(8,128)(2,1)}, u32[]{:S(2)}, u32[]{:S(2)}) collective-permute-start(bf16[768,1024]{1,0:T(8,128)(2,1)} %collective-permute-done), channel_id=1, source_target_pairs={{0,4},{4,8},{8,12},{12,16},{16,20},{20,24},{24,28},{28,0},{1,5},{5... | collective-permute-start | bytes 4718600 | tf_op jit(solution)/shard_map/ppermute | solution.py:16
  52.5 44.0 %collective-permute-start.3 = (bf16[768,1024]{1,0:T(8,128)(2,1)}, bf16[768,1024]{1,0:T(8,128)(2,1)}, u32[]{:S(2)}, u32[]{:S(2)}) collective-permute-start(bf16[768,1024]{1,0:T(8,128)(2,1)} %collective-permute-done.1), channel_id=1, source_target_pairs={{0,28},{4,0},{8,4},{12,8},{16,12},{20,16},{24,20},{28,24},{1,29},{... | collective-permute-start | bytes 4718600 | tf_op jit(solution)/shard_map/ppermute | solution.py:19
  83.3 24.0 %collective-permute-start.4 = (bf16[768,1024]{1,0:T(8,128)(2,1)}, bf16[768,1024]{1,0:T(8,128)(2,1)}, u32[]{:S(2)}, u32[]{:S(2)}) collective-permute-start(bf16[768,1024]{1,0:T(8,128)(2,1)} %collective-permute-done.2), channel_id=1, source_target_pairs={{0,4},{4,8},{8,12},{12,16},{16,20},{20,24},{24,28},{28,0},{1,5},{5... | collective-permute-start | bytes 4718600 | tf_op jit(solution)/shard_map/ppermute | solution.py:16
  96.4 34.4 %collective-permute-start.5 = (bf16[768,1024]{1,0:T(8,128)(2,1)}, bf16[768,1024]{1,0:T(8,128)(2,1)S(1)}, u32[]{:S(2)}, u32[]{:S(2)}) collective-permute-start(bf16[768,1024]{1,0:T(8,128)(2,1)} %collective-permute-done.3), channel_id=1, source_target_pairs={{0,28},{4,0},{8,4},{12,8},{16,12},{20,16},{24,20},{28,24},{1,29},{... | collective-permute-start | bytes 4718600 | tf_op jit(solution)/shard_map/ppermute | solution.py:19
  107.3 30.8 %collective-permute-start.6 = (bf16[768,1024]{1,0:T(8,128)(2,1)}, bf16[768,1024]{1,0:T(8,128)(2,1)}, u32[]{:S(2)}, u32[]{:S(2)}) collective-permute-start(bf16[768,1024]{1,0:T(8,128)(2,1)} %collective-permute-done.4), channel_id=1, source_target_pairs={{0,4},{4,8},{8,12},{12,16},{16,20},{20,24},{24,28},{28,0},{1,5},{5... | collective-permute-start | bytes 4718600 | tf_op jit(solution)/shard_map/ppermute | solution.py:16
  132.2 18.1 %copy-start.9 = (s32[16,2]{0,1:T(2,128)S(1)}, s32[16,2]{0,1:T(2,128)}, u32[]{:S(2)}) copy-start(s32[16,2]{0,1:T(2,128)} %param.17) | copy-start | bytes 388
  132.2 45.0 %copy-start.3 = (bf16[16,6144]{1,0:T(8,128)(2,1)S(1)}, bf16[16,6144]{1,0:T(8,128)(2,1)}, u32[]{:S(2)}) copy-start(bf16[16,6144]{1,0:T(8,128)(2,1)} %param.15) | copy-start | bytes 589828
  150.3 90.1 %all-gather.4.cloned.1.call-start = ((), (), s32[]{:S(2)}) async-start(), calls=%async_computation.5 | async-start | bytes 5308416 | tf_op jit(solution)/shard_map/all_gather | solution.py:108
  150.8 26.4 %copy-start.7 = (s32[32]{0:T(128)}, s32[32]{0:T(128)S(1)}, u32[]{:S(2)}) copy-start(s32[32]{0:T(128)S(1)} %select_reduce_fusion) | copy-start | bytes 388
  202.2 126.0 %reduce-scatter.5.cloned.1.call-start = ((), (), s32[]{:S(2)}) async-start(), calls=%async_computation.6 | async-start | bytes 5308416 | tf_op jit(solution)/shard_map/reduce_scatter | solution.py:116
  250.6 84.3 %copy-start.6 = (s32[16,2]{1,0:T(8,128)S(1)}, s32[16,2]{1,0:T(8,128)}, u32[]{:S(2)}) copy-start(s32[16,2]{1,0:T(8,128)} %get-tuple-element.108) | copy-start | bytes 388
  250.6 84.4 %copy-start.10 = (f32[16,2]{0,1:T(2,128)S(1)}, f32[16,2]{0,1:T(2,128)}, u32[]{:S(2)}) copy-start(f32[16,2]{0,1:T(2,128)} %param.18) | copy-start | bytes 388
  250.6 84.4 %copy-start.8 = (s32[32]{0:T(128)S(1)}, s32[32]{0:T(128)}, u32[]{:S(2)}) copy-start(s32[32]{0:T(128)} %copy-done.7) | copy-start | bytes 388
  250.6 107.6 %copy-start.1 = (bf16[64,1024]{1,0:T(8,128)(2,1)S(1)}, bf16[64,1024]{1,0:T(8,128)(2,1)}, u32[]{:S(2)}) copy-start(bf16[64,1024]{1,0:T(8,128)(2,1)} %param.14) | copy-start | bytes 393220
  274.1 83.4 %copy-start.4 = (bf16[16,6144]{1,0:T(8,128)(2,1)S(1)}, bf16[16,6144]{1,0:T(8,128)(2,1)}, u32[]{:S(2)}) copy-start(bf16[16,6144]{1,0:T(8,128)(2,1)} %param.15) | copy-start | bytes 589828
  274.1 83.4 %copy-start.5 = (bf16[16,6144]{1,0:T(8,128)(2,1)S(1)}, bf16[16,6144]{1,0:T(8,128)(2,1)}, u32[]{:S(2)}) copy-start(bf16[16,6144]{1,0:T(8,128)(2,1)} %reduce-scatter.3.cloned.1.call-done) | copy-start | bytes 589828
  330.3 24.7 %all-to-all-start.1 = ((bf16[4,12,6144]{2,1,0:T(8,128)(2,1)}), bf16[4,12,6144]{2,1,0:T(8,128)(2,1)S(1)}, u32[]{:S(2)}, u32[]{:S(2)}) async-start(bf16[4,12,6144]{2,1,0:T(8,128)(2,1)} %reshape.93), calls=%async_computation.3 | async-start | bytes 1572864 | tf_op jit(solution)/shard_map/all_to_all | solution.py:123
Sparse Core Ops, SparseCore 0:
  9.3 38.9 all-gather.5
  150.4 26.7 reduce-scatter.2
  202.3 37.9 all-gather.3
  274.2 53.8 reduce-scatter.4
